TPU v7x, 128 devices: a whole 4x4x4 slice. The times are simulated.
128 devices in a mesh: section: 8 (over x_hi, z), seq: 16 (over x_lo, y, core).
Axes of the slice: x: 4 (x_hi: 2, x_lo: 2; x = x_hi * 2 + x_lo), y: 4, z: 4, core: 2. Of those that a mesh axis runs over, the one named last changes fastest.
Arguments:
- queries: bfloat16 [8, 1536, 6144], P('section', 'seq'), may hold values from -140 to 140
- keys: bfloat16 [8, 1536, 6144], P('section', 'seq'), may hold values from -7 to 7
- values: bfloat16 [8, 1536, 6144], P('section', 'seq'), may hold values from -24 to 24
- lengths: int32 [8], replicated, may hold values from 768 to 1536, as said below
- span_mask: int32 [8, 8], replicated, may hold values from 0 to 1, as said below
Outputs:
- shifted: bfloat16 [8, 1536, 6144], P('section', 'seq')
Inputs may be any that keep to these rules, and one draw needn't show every extreme that they name: `lengths`: each entry lies from 768 to 1536; some group has exactly 1536. `span_mask`: ones on the diagonal, zeros above it; a row s has ones only in columns s - 4 to s; row 7 has a one in column 3.
All inputs are finite; a program needn't handle non-finite values.
Results may differ from a plain program's by a relative error of at most 0.0065.
Values may be sent and summed in bfloat16 or wider, within the bound.
No kernel may reach another device: no remote copies, remote signals or barrier semaphores. Data moves between devices by JAX's collectives and lax.ppermute only.
A program may use at most 128 MiB of HBM per device.

v0:
```python
import jax
import jax.numpy as jnp
from jax import lax
from jax.experimental import pallas as pl
from jax.experimental.pallas import tpu as pltpu
from jax.sharding import PartitionSpec as P

HEAD = 128
LOG2E = 1.4426950408889634
BLOCK_Q = 384
KEY_STEP = 256
REACH = 5
CORES = 2


def attend(lengths, span_mask, place, got, other):
    groups = span_mask.shape[0]
    run = got.shape[2]
    runs = got.shape[0] // groups
    rows = runs * run
    span = CORES * rows
    sizes = [n for n in range(KEY_STEP, span + 1, KEY_STEP) if n >= span // 2]

    def kernel(len_ref, mask_ref, place_ref, got_ref, other_ref, o_ref, q_in, keys, values, ones, q, top, acc, sems):
        core = place_ref[1]
        by_run = (groups, runs, CORES, run, HEAD)
        keys_by_run, values_by_run = keys.reshape(by_run), values.reshape(by_run)

        def copies(c):
            here = pl.ds(c * runs, runs)
            pairs = (
                (got_ref.at[here, 0], q_in.at[c]),
                (got_ref.at[here, 1], keys_by_run.at[c, :, core]),
                (got_ref.at[here, 2], values_by_run.at[c, :, core]),
                (other_ref.at[here, 0], keys_by_run.at[c, :, 1 - core]),
                (other_ref.at[here, 1], values_by_run.at[c, :, 1 - core]),
            )
            return [pltpu.make_async_copy(src, dst, sems.at[c, i]) for i, (src, dst) in enumerate(pairs)]

        def start(c, carry):
            for copy in copies(c):
                copy.start()
            return carry

        def clean(c):
            count = len_ref[c]
            base = (count - 1) // KEY_STEP * KEY_STEP
            here = pl.ds(pl.multiple_of(c * span + base, KEY_STEP), KEY_STEP)
            live = (base + lax.broadcasted_iota(jnp.int32, (KEY_STEP, HEAD), 0)) < count
            first = keys[pl.ds(pl.multiple_of(c * span, KEY_STEP), 16), :][0:1]
            keys[here, :] = jnp.where(live, keys[here, :], first)
            values[here, :] = jnp.where(live, values[here, :], jnp.bfloat16(0))
            ones[here, :] = jnp.where(live, jnp.bfloat16(1), jnp.bfloat16(0))

        def step(c, n, fresh):
            here = pl.ds(pl.multiple_of(c * span, KEY_STEP), n)
            k = keys[here, :]
            k = jnp.concatenate([k, k], axis=1)
            v = jnp.concatenate([values[here, :], ones[here, :]], axis=1)

            def scores(i):
                return lax.dot_general(
                    q[i * BLOCK_Q : (i + 1) * BLOCK_Q, :],
                    k,
                    (((1,), (1,)), ((), ())),
                    preferred_element_type=jnp.float32,
                )

            later = scores(0)
            for i in range(rows // BLOCK_Q):
                block = slice(i * BLOCK_Q, (i + 1) * BLOCK_Q)
                score = later
                if i + 1 < rows // BLOCK_Q:
                    later = scores(i + 1)
                new_top = jnp.max(score, axis=1, keepdims=True)
                if not fresh:
                    old_top = top[block, 0:1]
                    new_top = jnp.maximum(old_top, new_top)
                weight = jnp.exp2(score - new_top).astype(jnp.bfloat16)
                update = jnp.dot(weight, v, preferred_element_type=jnp.float32)
                if fresh:
                    acc[block, :] = update
                else:
                    acc[block, :] = acc[block, :] * jnp.exp2(old_top - new_top) + update
                top[block, :] = jnp.broadcast_to(new_top, (BLOCK_Q, HEAD))

        def by_length(c, fresh):
            steps = (len_ref[c] + KEY_STEP - 1) // KEY_STEP
            for n in sizes:
                pl.when(steps == n // KEY_STEP)(lambda n=n: step(c, n, fresh))

        def one_group(s, carry):
            for copy in copies(s):
                copy.wait()
            clean(s)
            scaled = q_in[s].reshape(rows, HEAD).astype(jnp.float32) * (LOG2E * HEAD**-0.5)
            high = scaled.astype(jnp.bfloat16)
            q[:, :HEAD] = high
            q[:, HEAD:] = (scaled - high.astype(jnp.float32)).astype(jnp.bfloat16)
            by_length(s, True)

            def earlier(c, inner):
                pl.when(mask_ref[s, c] > 0)(lambda: by_length(c, False))
                return inner

            lax.fori_loop(jnp.maximum(s - (REACH - 1), 0), s, earlier, 0)
            total = acc[...]
            o_ref[lax.rem(s + 1, groups)] = (total[:, :HEAD] / total[:, HEAD:]).astype(jnp.bfloat16)
            return carry

        @pl.when(place_ref[0] > 0)
        def _():
            lax.fori_loop(0, groups, start, 0)
            ones[...] = jnp.ones(ones.shape, jnp.bfloat16)
            lax.fori_loop(0, groups, one_group, 0)

    smem = pl.BlockSpec(memory_space=pltpu.SMEM)
    where_it_is = pl.BlockSpec(memory_space=pl.ANY)
    bf16, f32 = jnp.bfloat16, jnp.float32
    return pl.pallas_call(
        kernel,
        out_shape=jax.ShapeDtypeStruct((groups, rows, HEAD), bf16),
        in_specs=[smem] * 3 + [where_it_is] * 2,
        out_specs=pl.BlockSpec(memory_space=pltpu.VMEM),
        scratch_shapes=[
            pltpu.VMEM((groups, runs, run, HEAD), bf16),
            pltpu.VMEM((groups * span, HEAD), bf16),
            pltpu.VMEM((groups * span, HEAD), bf16),
            pltpu.VMEM((groups * span, HEAD), bf16),
            pltpu.VMEM((rows, 2 * HEAD), bf16),
            pltpu.VMEM((rows, HEAD), f32),
            pltpu.VMEM((rows, 2 * HEAD), f32),
            pltpu.SemaphoreType.DMA((groups, 5)),
        ],
        compiler_params=pltpu.CompilerParams(vmem_limit_bytes=48 * 2**20),
        name="attend",
    )(lengths, span_mask, place, got, other)


CHIPS = ("xh", "z", "xl", "y")


def body(queries, keys, values, lengths, span_mask):
    tokens, width = queries.shape[1:]
    heads = width // HEAD
    chips = lax.axis_size(CHIPS)
    core = lax.axis_index("core")

    def by_head(array):
        return jnp.transpose(array[0].reshape(tokens, heads, HEAD), (1, 0, 2))

    sent = jnp.stack([by_head(queries), by_head(keys), by_head(values)], axis=1)
    sent = jnp.pad(sent, ((0, chips - heads), (0, 0), (0, 0), (0, 0)))
    got = lax.all_to_all(sent, CHIPS, 0, 0, tiled=True)

    other = lax.ppermute(got[:, 1:], "core", [(0, 1), (1, 0)])
    active = (lax.axis_index(CHIPS) < heads).astype(jnp.int32)
    out = attend(lengths, span_mask, jnp.stack([active, core]), got, other)
    back = lax.all_to_all(out.reshape(chips, tokens, HEAD), CHIPS, 0, 0, tiled=True)[:heads]
    return jnp.transpose(back, (1, 0, 2)).reshape(1, tokens, width)


def solution(mesh):
    fine = jax.sharding.Mesh(mesh.devices.reshape(2, 4, 2, 4, 2), ("xh", "z", "xl", "y", "core"))
    spec = P(("xh", "z"), ("xl", "y", "core"), None)
    return jax.shard_map(
        body,
        mesh=fine,
        in_specs=(spec, spec, spec, P(), P()),
        out_specs=spec,
        check_vma=False,
    )
```

profile of v0, /device:TPU:0, one launch (start us, length us, event | category | flops | bytes accessed | tf_op | source)
XLA Modules:
  0.0 147.9 jit_solution(8684484388524092621)
XLA Ops:
  0.0 1.5 %copy.11 = bf16[12,8,48,128]{3,2,1,0:T(8,128)(2,1)S(1)} copy(bf16[12,8,48,128]{3,1,2,0:T(8,128)(2,1)} %bitcast.32) | data formatting | bytes 2359296
  1.5 0.0 copy-start.3
  1.5 0.3 copy.17
  1.8 0.0 copy-start.4
  1.8 0.9 copy-done.3
  2.8 0.2 copy.12
  3.0 0.2 copy-done.4
  3.2 0.2 copy.13
  3.4 0.6 copy_bitcast_fusion
  4.0 0.9 fusion.4
  5.0 70.2 %all_to_all.10.got_ref = bf16[64,3,96,128]{3,2,1,0:T(8,128)(2,1)S(1)} all-to-all(bf16[64,3,96,128]{3,2,1,0:T(8,128)(2,1)S(1)} %fusion.4), channel_id=1, replica_groups=mesh['xh'=2,'z'=4,'xl'=2,'y'=4,'core'=2] {'xh','z','xl','y'}, dimensions={0} | all-to-all | bytes 9437184 | tf_op jit(solution)/shard_map/all_to_all | solution.py:154
  75.2 0.0 copy-start.2
  75.2 0.0 copy-start
  75.2 0.0 copy-start.1
  75.2 2.4 %slice.8 = bf16[64,2,96,128]{3,2,1,0:T(8,128)(2,1)} slice(bf16[64,3,96,128]{3,2,1,0:T(8,128)(2,1)S(1)} %all_to_all.10.got_ref), slice={[0:64], [1:3], [0:96], [0:128]} | slice | bytes 6291456 | tf_op jit(solution)/shard_map/slice | solution.py:156
  77.6 0.7 copy-done.2
  78.3 0.0 collective-permute-start
  78.3 0.1 pad_add_fusion.place_ref
  78.4 5.8 %collective-permute-done.other_ref = bf16[64,2,96,128]{3,2,1,0:T(8,128)(2,1)S(1)} collective-permute-done((bf16[64,2,96,128]{3,2,1,0:T(8,128)(2,1)}, bf16[64,2,96,128]{3,2,1,0:T(8,128)(2,1)S(1)}, u32[]{:S(2)}, u32[]{:S(2)}) %collective-permute-start) | collective-permute-done | bytes 3145760 | tf_op jit(solution)/shard_map/ppermute | solution.py:156
  84.2 0.0 copy-done
  84.2 0.0 copy-done.1
  84.2 29.7 %attend.1 = bf16[8,768,128]{2,1,0:T(8,128)(2,1)S(1)} custom-call(s32[8]{0:T(128)S(1)} %copy-done.1, s32[8,8]{1,0:T(8,128)S(1)} %copy-done, s32[2]{0:T(128)S(1)} %pad_add_fusion.place_ref, bf16[64,3,96,128]{3,2,1,0:T(8,128)(2,1)} %copy-done.2, bf16[64,2,96,128]{3,2,1,0:T(8,128)(2,1)S(1)} %collective-permute-done.other_ref), custom_call_target="tpu_custom_call" | custom-call | tf_op jit(solution)/shard_map/attend/pallas_call | solution.py:120
  113.9 32.1 %all_to_all.11 = bf16[64,96,128]{2,1,0:T(8,128)(2,1)S(1)} all-to-all(bf16[64,96,128]{2,1,0:T(8,128)(2,1)S(1)} %bitcast.27), channel_id=1, replica_groups=mesh['xh'=2,'z'=4,'xl'=2,'y'=4,'core'=2] {'xh','z','xl','y'}, dimensions={0} | all-to-all | bytes 3145728 | tf_op jit(solution)/shard_map/all_to_all | solution.py:159
  146.0 0.1 slice_bitcast_fusion
  146.1 0.5 copy.10
  146.6 1.4 reshape.7
Async XLA Ops:
  1.5 1.3 copy-start.3
  1.8 1.4 copy-start.4
  75.2 3.1 %copy-start.2 = (bf16[64,3,96,128]{3,2,1,0:T(8,128)(2,1)}, bf16[64,3,96,128]{3,2,1,0:T(8,128)(2,1)S(1)}, u32[]{:S(2)}) copy-start(bf16[64,3,96,128]{3,2,1,0:T(8,128)(2,1)S(1)} %all_to_all.10.got_ref) | copy-start | bytes 14155780
  75.2 8.9 %copy-start = (s32[8,8]{1,0:T(8,128)S(1)}, s32[8,8]{1,0:T(8,128)}, u32[]{:S(2)}) copy-start(s32[8,8]{1,0:T(8,128)} %mask_ref.1) | copy-start | bytes 772
  75.2 8.9 %copy-start.1 = (s32[8]{0:T(128)S(1)}, s32[8]{0:T(128)}, u32[]{:S(2)}) copy-start(s32[8]{0:T(128)} %len_ref.1) | copy-start | bytes 100
  78.3 5.9 %collective-permute-start = (bf16[64,2,96,128]{3,2,1,0:T(8,128)(2,1)}, bf16[64,2,96,128]{3,2,1,0:T(8,128)(2,1)S(1)}, u32[]{:S(2)}, u32[]{:S(2)}) collective-permute-start(bf16[64,2,96,128]{3,2,1,0:T(8,128)(2,1)} %slice.8), channel_id=1, source_target_pairs={{0,1},{1,0},{2,3},{3,2},{4,5},{5,4},{6,7},{7,6},{8,9},{9,8},{10,11... | collective-permute-start | bytes 9437192 | tf_op jit(solution)/shard_map/ppermute | solution.py:156
where the time goes:
time: 150 us; the launch traced here: 148 us
  blocking collectives  102 us (68%)
  Pallas kernels  29.7 us (20%)
  local copies, waits for them, and re-layouts  8.94 us (6%)
  waiting for transfers between devices  5.79 us (4%)
    all_to_all x1, blocking collectives, body(): got = lax.all_to_all(sent, CHIPS, 0, 0, tiled=True)  70.2 us
    all_to_all x1, blocking collectives, body(): lax.all_to_all(out.reshape(chips, tokens, HEAD), CHIPS, 0, 0, tiled=True)  32.1 us
    pallas_call x1, Pallas kernels, attend(): pl.pallas_call(kernel, out_shape=jax.ShapeDtypeStruct((groups, rows, HEAD...  29.7 us
    ppermute x1, waiting for transfers between devices, body(): other = lax.ppermute(got[:, 1:], 'core', [(0, 1), (1, 0)])  5.79 us
    unnamed x13, local copies, waits for them, and re-layouts  3.76 us
  transfers between devices with their start and end apart: 1, of which 1 were waited for; matrix products, arithmetic and copies ran while one was open for 0% of the time, Pallas kernels for 0%

commit v1 on v0

--- a/solution.py
+++ b/solution.py
@@ -13,7 +13,28 @@
 CORES = 2
 
 
-def attend(lengths, span_mask, place, got, other):
+def pack(queries, keys, values, slots):
+    _, tokens, width = queries.shape
+    parts = 4
+    here = width // parts
+
+    def kernel(q_ref, k_ref, v_ref, o_ref):
+        for i, ref in enumerate((q_ref, k_ref, v_ref)):
+            for h in range(here // HEAD):
+                o_ref[h, i] = ref[0, :, h * HEAD : (h + 1) * HEAD]
+
+    return pl.pallas_call(
+        kernel,
+        grid=(parts,),
+        out_shape=jax.ShapeDtypeStruct((slots, 3, tokens, HEAD), queries.dtype),
+        in_specs=[pl.BlockSpec((1, tokens, here), lambda g: (0, 0, g))] * 3,
+        out_specs=pl.BlockSpec((here // HEAD, 3, tokens, HEAD), lambda g: (g, 0, 0, 0)),
+        compiler_params=pltpu.CompilerParams(vmem_limit_bytes=32 * 2**20),
+        name="pack",
+    )(queries, keys, values)
+
+
+def attend(lengths, span_mask, place, got, other_keys, other_values):
     groups = span_mask.shape[0]
     run = got.shape[2]
     runs = got.shape[0] // groups
@@ -21,7 +42,7 @@
     span = CORES * rows
     sizes = [n for n in range(KEY_STEP, span + 1, KEY_STEP) if n >= span // 2]
 
-    def kernel(len_ref, mask_ref, place_ref, got_ref, other_ref, o_ref, q_in, keys, values, ones, q, top, acc, sems):
+    def kernel(len_ref, mask_ref, place_ref, got_ref, other_k_ref, other_v_ref, o_ref, q_in, keys, values, ones, q, top, acc, sems):
         core = place_ref[1]
         by_run = (groups, runs, CORES, run, HEAD)
         keys_by_run, values_by_run = keys.reshape(by_run), values.reshape(by_run)
@@ -32,8 +53,8 @@
                 (got_ref.at[here, 0], q_in.at[c]),
                 (got_ref.at[here, 1], keys_by_run.at[c, :, core]),
                 (got_ref.at[here, 2], values_by_run.at[c, :, core]),
-                (other_ref.at[here, 0], keys_by_run.at[c, :, 1 - core]),
-                (other_ref.at[here, 1], values_by_run.at[c, :, 1 - core]),
+                (other_k_ref.at[here], keys_by_run.at[c, :, 1 - core]),
+                (other_v_ref.at[here], values_by_run.at[c, :, 1 - core]),
             )
             return [pltpu.make_async_copy(src, dst, sems.at[c, i]) for i, (src, dst) in enumerate(pairs)]
 
@@ -120,7 +141,7 @@
     return pl.pallas_call(
         kernel,
         out_shape=jax.ShapeDtypeStruct((groups, rows, HEAD), bf16),
-        in_specs=[smem] * 3 + [where_it_is] * 2,
+        in_specs=[smem] * 3 + [where_it_is] * 3,
         out_specs=pl.BlockSpec(memory_space=pltpu.VMEM),
         scratch_shapes=[
             pltpu.VMEM((groups, runs, run, HEAD), bf16),
@@ -134,7 +155,7 @@
         ],
         compiler_params=pltpu.CompilerParams(vmem_limit_bytes=48 * 2**20),
         name="attend",
-    )(lengths, span_mask, place, got, other)
+    )(lengths, span_mask, place, got, other_keys, other_values)
 
 
 CHIPS = ("xh", "z", "xl", "y")
@@ -146,16 +167,14 @@
     chips = lax.axis_size(CHIPS)
     core = lax.axis_index("core")
 
-    def by_head(array):
-        return jnp.transpose(array[0].reshape(tokens, heads, HEAD), (1, 0, 2))
-
-    sent = jnp.stack([by_head(queries), by_head(keys), by_head(values)], axis=1)
-    sent = jnp.pad(sent, ((0, chips - heads), (0, 0), (0, 0), (0, 0)))
+    sent = pack(queries, keys, values, chips)
     got = lax.all_to_all(sent, CHIPS, 0, 0, tiled=True)
 
-    other = lax.ppermute(got[:, 1:], "core", [(0, 1), (1, 0)])
+    rest, own_keys = lax.optimization_barrier((got, got[:, 1]))
+    other_keys = lax.ppermute(own_keys, "core", [(0, 1), (1, 0)])
+    other_values = lax.ppermute(rest[:, 2], "core", [(0, 1), (1, 0)])
     active = (lax.axis_index(CHIPS) < heads).astype(jnp.int32)
-    out = attend(lengths, span_mask, jnp.stack([active, core]), got, other)
+    out = attend(lengths, span_mask, jnp.stack([active, core]), got, other_keys, other_values)
     back = lax.all_to_all(out.reshape(chips, tokens, HEAD), CHIPS, 0, 0, tiled=True)[:heads]
     return jnp.transpose(back, (1, 0, 2)).reshape(1, tokens, width)
 

time: 150 us -> 153 us (1.020)
  Pallas kernels: 29.7 us -> 33.5 us
    pallas_call x0 -> x1, Pallas kernels: none -> 2.65 us  [pack(): pl.pallas_call(kernel, grid=(parts,), out_shape=jax.ShapeDtypeStruct((slo...]
    squeeze x0 -> x2, local copies, waits for them, and re-layouts: none -> 2.59 us  [the longest x1 1.34 us: body(): rest, own_keys = lax.optimization_barrier((got, got[:, 1]))]
    slice x1 -> x0, local copies, waits for them, and re-layouts: 2.38 us -> none  [body(): other = lax.ppermute(got[:, 1:], 'core', [(0, 1), (1, 0)])]
    unnamed x13 -> x12, local copies, waits for them, and re-layouts: 3.76 us -> 4.31 us
    ppermute x1 -> x2, waiting for transfers between devices: 5.79 us -> 5.28 us  [the longest x1 3.03 us: body(): other_values = lax.ppermute(rest[:, 2], 'core', [(0, 1), (1, 0)])]
  transfers between devices with their start and end apart: 1 -> 2, of which waited for: 1 -> 2; matrix products, arithmetic and copies ran while one was open for 0% -> 0% of each run, Pallas kernels for 0% -> 0%
where the time goes in v1:
time: 153 us; the launch traced here: 151 us
  blocking collectives  102 us (67%)
  Pallas kernels  33.5 us (22%)
  local copies, waits for them, and re-layouts  8.78 us (6%)
  waiting for transfers between devices  5.28 us (3%)
    all_to_all x1, blocking collectives, body(): got = lax.all_to_all(sent, CHIPS, 0, 0, tiled=True)  70.2 us
    all_to_all x1, blocking collectives, body(): lax.all_to_all(out.reshape(chips, tokens, HEAD), CHIPS, 0, 0, tiled=True)  32.1 us
    pallas_call x1, Pallas kernels, attend(): pl.pallas_call(kernel, out_shape=jax.ShapeDtypeStruct((groups, rows, HEAD...  30.9 us
    unnamed x12, local copies, waits for them, and re-layouts  4.31 us
  transfers between devices with their start and end apart: 2, of which 2 were waited for; matrix products, arithmetic and copies ran while one was open for 0% of the time, Pallas kernels for 0%

profile of v1, /device:TPU:0, one launch (start us, length us, event | category | flops | bytes accessed | tf_op | source)
XLA Modules:
  0.0 150.6 jit_solution(10740232974344227886)
XLA Ops:
  0.0 0.0 copy-start
  0.0 1.3 copy-done
  1.3 0.0 copy-start.1
  1.3 1.3 copy-done.1
  2.5 0.0 copy-start.2
  2.5 1.3 copy-done.2
  3.8 2.7 %pack.1 = bf16[64,3,96,128]{3,2,1,0:T(8,128)(2,1)S(1)} custom-call(bf16[1,96,6144]{2,1,0:T(8,128)(2,1)S(1)} %copy-done, bf16[1,96,6144]{2,1,0:T(8,128)(2,1)S(1)} %copy-done.1, bf16[1,96,6144]{2,1,0:T(8,128)(2,1)S(1)} %copy-done.2), custom_call_target="tpu_custom_call" | custom-call | tf_op jit(solution)/shard_map/pack/pallas_call | solution.py:26
  6.5 70.2 %all_to_all.10.got_ref = bf16[64,3,96,128]{3,2,1,0:T(8,128)(2,1)S(1)} all-to-all(bf16[64,3,96,128]{3,2,1,0:T(8,128)(2,1)S(1)} %pack.1), channel_id=1, replica_groups=mesh['xh'=2,'z'=4,'xl'=2,'y'=4,'core'=2] {'xh','z','xl','y'}, dimensions={0} | all-to-all | bytes 9437184 | tf_op jit(solution)/shard_map/all_to_all | solution.py:171
  76.7 0.0 copy-start.5
  76.7 1.3 slice_bitcast_fusion.1
  78.1 0.0 copy-start.3
  78.1 0.0 copy-start.4
  78.1 1.2 slice_bitcast_fusion
  79.3 0.5 copy-done.5
  79.8 0.0 collective-permute-start.1
  79.8 0.5 collective-permute-start
  80.3 0.1 pad_add_fusion.place_ref
  80.4 3.0 %collective-permute-done.1.other_v_ref = bf16[64,96,128]{2,1,0:T(8,128)(2,1)S(1)} collective-permute-done((bf16[64,96,128]{2,1,0:T(8,128)(2,1)}, bf16[64,96,128]{2,1,0:T(8,128)(2,1)S(1)}, u32[]{:S(2)}, u32[]{:S(2)}) %collective-permute-start.1) | collective-permute-done | bytes 1572896 | tf_op jit(solution)/shard_map/ppermute | solution.py:175
  83.4 2.2 %collective-permute-done.other_k_ref = bf16[64,96,128]{2,1,0:T(8,128)(2,1)S(1)} collective-permute-done((bf16[64,96,128]{2,1,0:T(8,128)(2,1)}, bf16[64,96,128]{2,1,0:T(8,128)(2,1)S(1)}, u32[]{:S(2)}, u32[]{:S(2)}) %collective-permute-start) | collective-permute-done | bytes 1572896 | tf_op jit(solution)/shard_map/ppermute | solution.py:174
  85.7 0.0 copy-done.3
  85.7 0.0 copy-done.4
  85.7 30.9 %attend.1 = bf16[8,768,128]{2,1,0:T(8,128)(2,1)S(1)} custom-call(s32[8]{0:T(128)S(1)} %copy-done.4, s32[8,8]{1,0:T(8,128)S(1)} %copy-done.3, s32[2]{0:T(128)S(1)} %pad_add_fusion.place_ref, bf16[64,3,96,128]{3,2,1,0:T(8,128)(2,1)} %copy-done.5, bf16[64,96,128]{2,1,0:T(8,128)(2,1)S(1)} %collective-permute-done.other_k_ref, ...), custom_call_target="tpu_custom_call" | custom-call | tf_op jit(solution)/shard_map/attend/pallas_call | solution.py:141
  116.6 32.1 %all_to_all.11 = bf16[64,96,128]{2,1,0:T(8,128)(2,1)S(1)} all-to-all(bf16[64,96,128]{2,1,0:T(8,128)(2,1)S(1)} %bitcast.11), channel_id=1, replica_groups=mesh['xh'=2,'z'=4,'xl'=2,'y'=4,'core'=2] {'xh','z','xl','y'}, dimensions={0} | all-to-all | bytes 3145728 | tf_op jit(solution)/shard_map/all_to_all | solution.py:178
  148.7 0.1 slice_bitcast_fusion.2
  148.8 0.5 copy.11
  149.2 1.4 reshape.7
Async XLA Ops:
  0.0 1.3 copy-start
  1.3 1.3 copy-start.1
  2.5 1.3 copy-start.2
  76.7 3.1 %copy-start.5 = (bf16[64,3,96,128]{3,2,1,0:T(8,128)(2,1)}, bf16[64,3,96,128]{3,2,1,0:T(8,128)(2,1)S(1)}, u32[]{:S(2)}) copy-start(bf16[64,3,96,128]{3,2,1,0:T(8,128)(2,1)S(1)} %all_to_all.10.got_ref) | copy-start | bytes 14155780
  78.1 7.6 %copy-start.3 = (s32[8,8]{1,0:T(8,128)S(1)}, s32[8,8]{1,0:T(8,128)}, u32[]{:S(2)}) copy-start(s32[8,8]{1,0:T(8,128)} %mask_ref.1) | copy-start | bytes 772
  78.1 7.6 %copy-start.4 = (s32[8]{0:T(128)S(1)}, s32[8]{0:T(128)}, u32[]{:S(2)}) copy-start(s32[8]{0:T(128)} %len_ref.1) | copy-start | bytes 100
  79.8 3.6 %collective-permute-start.1 = (bf16[64,96,128]{2,1,0:T(8,128)(2,1)}, bf16[64,96,128]{2,1,0:T(8,128)(2,1)S(1)}, u32[]{:S(2)}, u32[]{:S(2)}) collective-permute-start(bf16[64,96,128]{2,1,0:T(8,128)(2,1)} %slice_bitcast_fusion), channel_id=1, source_target_pairs={{0,1},{1,0},{2,3},{3,2},{4,5},{5,4},{6,7},{7,6},{8,9},{9,8},{10,11... | collective-permute-start | bytes 4718600 | tf_op jit(solution)/shard_map/ppermute | solution.py:175
  79.8 5.9 %collective-permute-start = (bf16[64,96,128]{2,1,0:T(8,128)(2,1)}, bf16[64,96,128]{2,1,0:T(8,128)(2,1)S(1)}, u32[]{:S(2)}, u32[]{:S(2)}) collective-permute-start(bf16[64,96,128]{2,1,0:T(8,128)(2,1)} %slice_bitcast_fusion.1), channel_id=1, source_target_pairs={{0,1},{1,0},{2,3},{3,2},{4,5},{5,4},{6,7},{7,6},{8,9},{9,8},{10,11... | collective-permute-start | bytes 4718600 | tf_op jit(solution)/shard_map/ppermute | solution.py:174

commit v2 on v0

--- a/solution.py
+++ b/solution.py
@@ -11,6 +11,48 @@
 KEY_STEP = 256
 REACH = 5
 CORES = 2
+
+
+def pack(queries, keys, values, slots):
+    _, tokens, width = queries.shape
+    parts = 4
+    here = width // parts
+    heads = here // HEAD
+
+    def kernel(q_ref, k_ref, v_ref, o_ref, held, ready, in_sems, out_sems):
+        def load(g, i):
+            columns = slice(g * here, (g + 1) * here)
+            return pltpu.make_async_copy((q_ref, k_ref, v_ref)[i].at[0, :, columns], held.at[g, i], in_sems.at[g, i])
+
+        def store(g):
+            return pltpu.make_async_copy(ready.at[g], o_ref.at[pl.ds(g * heads, heads)], out_sems.at[g])
+
+        for g in range(parts):
+            for i in range(3):
+                load(g, i).start()
+        for g in range(parts):
+            for i in range(3):
+                load(g, i).wait()
+                for h in range(heads):
+                    ready[g, h, i] = held[g, i, :, h * HEAD : (h + 1) * HEAD]
+            store(g).start()
+        for g in range(parts):
+            store(g).wait()
+
+    return pl.pallas_call(
+        kernel,
+        out_shape=jax.ShapeDtypeStruct((slots, 3, tokens, HEAD), queries.dtype),
+        in_specs=[pl.BlockSpec(memory_space=pl.ANY)] * 3,
+        out_specs=pl.BlockSpec(memory_space=pl.ANY),
+        scratch_shapes=[
+            pltpu.VMEM((parts, 3, tokens, here), queries.dtype),
+            pltpu.VMEM((parts, heads, 3, tokens, HEAD), queries.dtype),
+            pltpu.SemaphoreType.DMA((parts, 3)),
+            pltpu.SemaphoreType.DMA((parts,)),
+        ],
+        compiler_params=pltpu.CompilerParams(vmem_limit_bytes=56 * 2**20),
+        name="pack",
+    )(queries, keys, values)
 
 
 def attend(lengths, span_mask, place, got, other):
@@ -146,11 +188,7 @@
     chips = lax.axis_size(CHIPS)
     core = lax.axis_index("core")
 
-    def by_head(array):
-        return jnp.transpose(array[0].reshape(tokens, heads, HEAD), (1, 0, 2))
-
-    sent = jnp.stack([by_head(queries), by_head(keys), by_head(values)], axis=1)
-    sent = jnp.pad(sent, ((0, chips - heads), (0, 0), (0, 0), (0, 0)))
+    sent = pack(queries, keys, values, chips)
     got = lax.all_to_all(sent, CHIPS, 0, 0, tiled=True)
 
     other = lax.ppermute(got[:, 1:], "core", [(0, 1), (1, 0)])

time: 150 us -> 150 us (level)
  Pallas kernels: 29.7 us -> 34.3 us
  local copies, waits for them, and re-layouts: 8.94 us -> 4.94 us
    unnamed x13 -> x6, local copies, waits for them, and re-layouts: 3.76 us -> 0.66 us
    pallas_call x0 -> x1, Pallas kernels: none -> 3.08 us  [pack(): pl.pallas_call(kernel, out_shape=jax.ShapeDtypeStruct((slots, 3, tokens,...]
where the time goes in v2:
time: 150 us; the launch traced here: 148 us
  blocking collectives  103 us (69%)
  Pallas kernels  34.3 us (23%)
  waiting for transfers between devices  5.79 us (4%)
  local copies, waits for them, and re-layouts  4.94 us (3%)
    all_to_all x1, blocking collectives, body(): got = lax.all_to_all(sent, CHIPS, 0, 0, tiled=True)  70.5 us
    all_to_all x1, blocking collectives, body(): lax.all_to_all(out.reshape(chips, tokens, HEAD), CHIPS, 0, 0, tiled=True)  32.2 us
    pallas_call x1, Pallas kernels, attend(): pl.pallas_call(kernel, out_shape=jax.ShapeDtypeStruct((groups, rows, HEAD...  31.2 us
    ppermute x1, waiting for transfers between devices, body(): other = lax.ppermute(got[:, 1:], 'core', [(0, 1), (1, 0)])  5.79 us
    pallas_call x1, Pallas kernels, pack(): pl.pallas_call(kernel, out_shape=jax.ShapeDtypeStruct((slots, 3, tokens,...  3.08 us
  transfers between devices with their start and end apart: 1, of which 1 were waited for; matrix products, arithmetic and copies ran while one was open for 0% of the time, Pallas kernels for 0%

profile of v2, /device:TPU:0, one launch (start us, length us, event | category | flops | bytes accessed | tf_op | source)
XLA Modules:
  0.0 147.7 jit_solution(10033849155636187424)
XLA Ops:
  0.0 3.1 %pack.1 = bf16[64,3,96,128]{3,2,1,0:T(8,128)(2,1)} custom-call(bf16[1,96,6144]{2,1,0:T(8,128)(2,1)} %q_ref.1, bf16[1,96,6144]{2,1,0:T(8,128)(2,1)} %k_ref.1, bf16[1,96,6144]{2,1,0:T(8,128)(2,1)} %v_ref.1), custom_call_target="tpu_custom_call" | custom-call | tf_op jit(solution)/shard_map/pack/pallas_call | solution.py:42
  3.1 70.5 %all_to_all.10.got_ref = bf16[64,3,96,128]{3,2,1,0:T(8,128)(2,1)S(1)} all-to-all(bf16[64,3,96,128]{3,2,1,0:T(8,128)(2,1)} %pack.1), channel_id=1, replica_groups=mesh['xh'=2,'z'=4,'xl'=2,'y'=4,'core'=2] {'xh','z','xl','y'}, dimensions={0} | all-to-all | bytes 9437184 | tf_op jit(solution)/shard_map/all_to_all | solution.py:192
  73.5 0.0 copy-start.2
  73.5 0.0 copy-start
  73.5 0.0 copy-start.1
  73.6 2.4 %slice.8 = bf16[64,2,96,128]{3,2,1,0:T(8,128)(2,1)} slice(bf16[64,3,96,128]{3,2,1,0:T(8,128)(2,1)S(1)} %all_to_all.10.got_ref), slice={[0:64], [1:3], [0:96], [0:128]} | slice | bytes 6291456 | tf_op jit(solution)/shard_map/slice | solution.py:194
  75.9 0.7 copy-done.2
  76.6 0.0 collective-permute-start
  76.6 0.1 pad_add_fusion.place_ref
  76.7 5.8 %collective-permute-done.other_ref = bf16[64,2,96,128]{3,2,1,0:T(8,128)(2,1)S(1)} collective-permute-done((bf16[64,2,96,128]{3,2,1,0:T(8,128)(2,1)}, bf16[64,2,96,128]{3,2,1,0:T(8,128)(2,1)S(1)}, u32[]{:S(2)}, u32[]{:S(2)}) %collective-permute-start) | collective-permute-done | bytes 3145760 | tf_op jit(solution)/shard_map/ppermute | solution.py:194
  82.5 0.0 copy-done
  82.5 0.0 copy-done.1
  82.5 31.2 %attend.1 = bf16[8,768,128]{2,1,0:T(8,128)(2,1)S(1)} custom-call(s32[8]{0:T(128)S(1)} %copy-done.1, s32[8,8]{1,0:T(8,128)S(1)} %copy-done, s32[2]{0:T(128)S(1)} %pad_add_fusion.place_ref, bf16[64,3,96,128]{3,2,1,0:T(8,128)(2,1)} %copy-done.2, bf16[64,2,96,128]{3,2,1,0:T(8,128)(2,1)S(1)} %collective-permute-done.other_ref), custom_call_target="tpu_custom_call" | custom-call | tf_op jit(solution)/shard_map/attend/pallas_call | solution.py:162
  113.7 32.2 %all_to_all.11 = bf16[64,96,128]{2,1,0:T(8,128)(2,1)S(1)} all-to-all(bf16[64,96,128]{2,1,0:T(8,128)(2,1)S(1)} %bitcast.5), channel_id=1, replica_groups=mesh['xh'=2,'z'=4,'xl'=2,'y'=4,'core'=2] {'xh','z','xl','y'}, dimensions={0} | all-to-all | bytes 3145728 | tf_op jit(solution)/shard_map/all_to_all | solution.py:197
  145.8 0.1 slice_bitcast_fusion
  145.9 0.5 copy.6
  146.4 1.4 reshape.7
Async XLA Ops:
  73.5 3.0 %copy-start.2 = (bf16[64,3,96,128]{3,2,1,0:T(8,128)(2,1)}, bf16[64,3,96,128]{3,2,1,0:T(8,128)(2,1)S(1)}, u32[]{:S(2)}) copy-start(bf16[64,3,96,128]{3,2,1,0:T(8,128)(2,1)S(1)} %all_to_all.10.got_ref) | copy-start | bytes 14155780
  73.5 8.9 %copy-start = (s32[8,8]{1,0:T(8,128)S(1)}, s32[8,8]{1,0:T(8,128)}, u32[]{:S(2)}) copy-start(s32[8,8]{1,0:T(8,128)} %mask_ref.1) | copy-start | bytes 772
  73.5 8.9 %copy-start.1 = (s32[8]{0:T(128)S(1)}, s32[8]{0:T(128)}, u32[]{:S(2)}) copy-start(s32[8]{0:T(128)} %len_ref.1) | copy-start | bytes 100
  76.6 5.9 %collective-permute-start = (bf16[64,2,96,128]{3,2,1,0:T(8,128)(2,1)}, bf16[64,2,96,128]{3,2,1,0:T(8,128)(2,1)S(1)}, u32[]{:S(2)}, u32[]{:S(2)}) collective-permute-start(bf16[64,2,96,128]{3,2,1,0:T(8,128)(2,1)} %slice.8), channel_id=1, source_target_pairs={{0,1},{1,0},{2,3},{3,2},{4,5},{5,4},{6,7},{7,6},{8,9},{9,8},{10,11... | collective-permute-start | bytes 9437192 | tf_op jit(solution)/shard_map/ppermute | solution.py:194

commit v3 on v2

--- a/solution.py
+++ b/solution.py
@@ -11,6 +11,21 @@
 KEY_STEP = 256
 REACH = 5
 CORES = 2
+WEIGHT_LIMIT = 2.0**60
+FIRST, KEEP, MOVE = range(3)
+
+
+def fold(weight):
+    best = weight[:, :HEAD]
+    for j in range(HEAD, weight.shape[1], HEAD):
+        best = jnp.maximum(best, weight[:, j : j + HEAD])
+    while best.shape[0] % 32 == 0:
+        half = best.shape[0] // 2
+        best = jnp.maximum(best[:half], best[half:])
+    tile = best[:16]
+    for j in range(16, best.shape[0], 16):
+        tile = jnp.maximum(tile, best[j : j + 16])
+    return tile
 
 
 def pack(queries, keys, values, slots):
@@ -63,7 +78,7 @@
     span = CORES * rows
     sizes = [n for n in range(KEY_STEP, span + 1, KEY_STEP) if n >= span // 2]
 
-    def kernel(len_ref, mask_ref, place_ref, got_ref, other_ref, o_ref, q_in, keys, values, ones, q, top, acc, sems):
+    def kernel(len_ref, mask_ref, place_ref, got_ref, other_ref, o_ref, q_in, keys, values, ones, q, top, acc, largest, sems):
         core = place_ref[1]
         by_run = (groups, runs, CORES, run, HEAD)
         keys_by_run, values_by_run = keys.reshape(by_run), values.reshape(by_run)
@@ -94,7 +109,7 @@
             values[here, :] = jnp.where(live, values[here, :], jnp.bfloat16(0))
             ones[here, :] = jnp.where(live, jnp.bfloat16(1), jnp.bfloat16(0))
 
-        def step(c, n, fresh):
+        def step(c, n, kind):
             here = pl.ds(pl.multiple_of(c * span, KEY_STEP), n)
             k = keys[here, :]
             k = jnp.concatenate([k, k], axis=1)
@@ -114,22 +129,28 @@
                 score = later
                 if i + 1 < rows // BLOCK_Q:
                     later = scores(i + 1)
+                if kind == KEEP:
+                    kept = jnp.concatenate([top[block, :]] * (n // HEAD), axis=1)
+                    weight = jnp.exp2(score - kept).astype(jnp.bfloat16)
+                    largest[...] = jnp.maximum(largest[...], fold(weight))
+                    acc[block, :] += jnp.dot(weight, v, preferred_element_type=jnp.float32)
+                    continue
                 new_top = jnp.max(score, axis=1, keepdims=True)
-                if not fresh:
+                if kind == MOVE:
                     old_top = top[block, 0:1]
                     new_top = jnp.maximum(old_top, new_top)
                 weight = jnp.exp2(score - new_top).astype(jnp.bfloat16)
                 update = jnp.dot(weight, v, preferred_element_type=jnp.float32)
-                if fresh:
+                if kind == FIRST:
                     acc[block, :] = update
                 else:
                     acc[block, :] = acc[block, :] * jnp.exp2(old_top - new_top) + update
                 top[block, :] = jnp.broadcast_to(new_top, (BLOCK_Q, HEAD))
 
-        def by_length(c, fresh):
+        def by_length(c, kind):
             steps = (len_ref[c] + KEY_STEP - 1) // KEY_STEP
             for n in sizes:
-                pl.when(steps == n // KEY_STEP)(lambda n=n: step(c, n, fresh))
+                pl.when(steps == n // KEY_STEP)(lambda n=n: step(c, n, kind))
 
         def one_group(s, carry):
             for copy in copies(s):
@@ -139,13 +160,24 @@
             high = scaled.astype(jnp.bfloat16)
             q[:, :HEAD] = high
             q[:, HEAD:] = (scaled - high.astype(jnp.float32)).astype(jnp.bfloat16)
-            by_length(s, True)
-
-            def earlier(c, inner):
-                pl.when(mask_ref[s, c] > 0)(lambda: by_length(c, False))
-                return inner
-
-            lax.fori_loop(jnp.maximum(s - (REACH - 1), 0), s, earlier, 0)
+
+            def attempt(state):
+                again, _ = state
+                by_length(s, FIRST)
+                largest[...] = jnp.zeros(largest.shape, jnp.bfloat16)
+
+                def earlier(c, inner):
+                    live = mask_ref[s, c] > 0
+                    pl.when(live & (again == 0))(lambda: by_length(c, KEEP))
+                    pl.when(live & (again > 0))(lambda: by_length(c, MOVE))
+                    return inner
+
+                lax.fori_loop(jnp.maximum(s - (REACH - 1), 0), s, earlier, 0)
+                over = jnp.max(largest[...].astype(jnp.float32)) > WEIGHT_LIMIT
+                return again + 1, over.astype(jnp.int32)
+
+            zero = jnp.int32(0)
+            lax.while_loop(lambda x: (x[0] == 0) | ((x[0] == 1) & (x[1] > 0)), attempt, (zero, zero))
             total = acc[...]
             o_ref[lax.rem(s + 1, groups)] = (total[:, :HEAD] / total[:, HEAD:]).astype(jnp.bfloat16)
             return carry
@@ -172,6 +204,7 @@
             pltpu.VMEM((rows, 2 * HEAD), bf16),
             pltpu.VMEM((rows, HEAD), f32),
             pltpu.VMEM((rows, 2 * HEAD), f32),
+            pltpu.VMEM((16, HEAD), bf16),
             pltpu.SemaphoreType.DMA((groups, 5)),
         ],
         compiler_params=pltpu.CompilerParams(vmem_limit_bytes=48 * 2**20),

time: 150 us -> 150 us (level); the launches traced: 148 us -> 153 us
  Pallas kernels: 34.3 us -> 39.1 us
    pallas_call x1, Pallas kernels: 31.2 us -> 36 us  [attend(): pl.pallas_call(kernel, out_shape=jax.ShapeDtypeStruct((groups, rows, HEAD...]
where the time goes in v3:
time: 150 us; the launch traced here: 153 us
  blocking collectives  103 us (69%)
  Pallas kernels  39.1 us (26%)
  waiting for transfers between devices  5.79 us (4%)
  local copies, waits for them, and re-layouts  4.94 us (3%)
    all_to_all x1, blocking collectives, body(): got = lax.all_to_all(sent, CHIPS, 0, 0, tiled=True)  70.5 us
    pallas_call x1, Pallas kernels, attend(): pl.pallas_call(kernel, out_shape=jax.ShapeDtypeStruct((groups, rows, HEAD...  36 us
    all_to_all x1, blocking collectives, body(): lax.all_to_all(out.reshape(chips, tokens, HEAD), CHIPS, 0, 0, tiled=True)  32.2 us
    ppermute x1, waiting for transfers between devices, body(): other = lax.ppermute(got[:, 1:], 'core', [(0, 1), (1, 0)])  5.79 us
    pallas_call x1, Pallas kernels, pack(): pl.pallas_call(kernel, out_shape=jax.ShapeDtypeStruct((slots, 3, tokens,...  3.08 us
  transfers between devices with their start and end apart: 1, of which 1 were waited for; matrix products, arithmetic and copies ran while one was open for 0% of the time, Pallas kernels for 0%

profile of v3, /device:TPU:0, one launch (start us, length us, event | category | flops | bytes accessed | tf_op | source)
XLA Modules:
  0.0 152.5 jit_solution(14474350211894767869)
XLA Ops:
  0.0 3.1 %pack.1 = bf16[64,3,96,128]{3,2,1,0:T(8,128)(2,1)} custom-call(bf16[1,96,6144]{2,1,0:T(8,128)(2,1)} %q_ref.1, bf16[1,96,6144]{2,1,0:T(8,128)(2,1)} %k_ref.1, bf16[1,96,6144]{2,1,0:T(8,128)(2,1)} %v_ref.1), custom_call_target="tpu_custom_call" | custom-call | tf_op jit(solution)/shard_map/pack/pallas_call | solution.py:57
  3.1 70.5 %all_to_all.10.got_ref = bf16[64,3,96,128]{3,2,1,0:T(8,128)(2,1)S(1)} all-to-all(bf16[64,3,96,128]{3,2,1,0:T(8,128)(2,1)} %pack.1), channel_id=1, replica_groups=mesh['xh'=2,'z'=4,'xl'=2,'y'=4,'core'=2] {'xh','z','xl','y'}, dimensions={0} | all-to-all | bytes 9437184 | tf_op jit(solution)/shard_map/all_to_all | solution.py:225
  73.5 0.0 copy-start.2
  73.5 0.0 copy-start
  73.5 0.0 copy-start.1
  73.6 2.4 %slice.8 = bf16[64,2,96,128]{3,2,1,0:T(8,128)(2,1)} slice(bf16[64,3,96,128]{3,2,1,0:T(8,128)(2,1)S(1)} %all_to_all.10.got_ref), slice={[0:64], [1:3], [0:96], [0:128]} | slice | bytes 6291456 | tf_op jit(solution)/shard_map/slice | solution.py:227
  75.9 0.7 copy-done.2
  76.6 0.0 collective-permute-start
  76.6 0.1 pad_add_fusion.place_ref
  76.7 5.8 %collective-permute-done.other_ref = bf16[64,2,96,128]{3,2,1,0:T(8,128)(2,1)S(1)} collective-permute-done((bf16[64,2,96,128]{3,2,1,0:T(8,128)(2,1)}, bf16[64,2,96,128]{3,2,1,0:T(8,128)(2,1)S(1)}, u32[]{:S(2)}, u32[]{:S(2)}) %collective-permute-start) | collective-permute-done | bytes 3145760 | tf_op jit(solution)/shard_map/ppermute | solution.py:227
  82.5 0.0 copy-done
  82.5 0.0 copy-done.1
  82.5 36.0 %attend.1 = bf16[8,768,128]{2,1,0:T(8,128)(2,1)S(1)} custom-call(s32[8]{0:T(128)S(1)} %copy-done.1, s32[8,8]{1,0:T(8,128)S(1)} %copy-done, s32[2]{0:T(128)S(1)} %pad_add_fusion.place_ref, bf16[64,3,96,128]{3,2,1,0:T(8,128)(2,1)} %copy-done.2, bf16[64,2,96,128]{3,2,1,0:T(8,128)(2,1)S(1)} %collective-permute-done.other_ref), custom_call_target="tpu_custom_call" | custom-call | tf_op jit(solution)/shard_map/attend/pallas_call | solution.py:194
  118.5 32.2 %all_to_all.11 = bf16[64,96,128]{2,1,0:T(8,128)(2,1)S(1)} all-to-all(bf16[64,96,128]{2,1,0:T(8,128)(2,1)S(1)} %bitcast.5), channel_id=1, replica_groups=mesh['xh'=2,'z'=4,'xl'=2,'y'=4,'core'=2] {'xh','z','xl','y'}, dimensions={0} | all-to-all | bytes 3145728 | tf_op jit(solution)/shard_map/all_to_all | solution.py:230
  150.6 0.1 slice_bitcast_fusion
  150.7 0.5 copy.6
  151.2 1.4 reshape.7
Async XLA Ops:
  73.5 3.0 %copy-start.2 = (bf16[64,3,96,128]{3,2,1,0:T(8,128)(2,1)}, bf16[64,3,96,128]{3,2,1,0:T(8,128)(2,1)S(1)}, u32[]{:S(2)}) copy-start(bf16[64,3,96,128]{3,2,1,0:T(8,128)(2,1)S(1)} %all_to_all.10.got_ref) | copy-start | bytes 14155780
  73.5 8.9 %copy-start = (s32[8,8]{1,0:T(8,128)S(1)}, s32[8,8]{1,0:T(8,128)}, u32[]{:S(2)}) copy-start(s32[8,8]{1,0:T(8,128)} %mask_ref.1) | copy-start | bytes 772
  73.5 8.9 %copy-start.1 = (s32[8]{0:T(128)S(1)}, s32[8]{0:T(128)}, u32[]{:S(2)}) copy-start(s32[8]{0:T(128)} %len_ref.1) | copy-start | bytes 100
  76.6 5.9 %collective-permute-start = (bf16[64,2,96,128]{3,2,1,0:T(8,128)(2,1)}, bf16[64,2,96,128]{3,2,1,0:T(8,128)(2,1)S(1)}, u32[]{:S(2)}, u32[]{:S(2)}) collective-permute-start(bf16[64,2,96,128]{3,2,1,0:T(8,128)(2,1)} %slice.8), channel_id=1, source_target_pairs={{0,1},{1,0},{2,3},{3,2},{4,5},{5,4},{6,7},{7,6},{8,9},{9,8},{10,11... | collective-permute-start | bytes 9437192 | tf_op jit(solution)/shard_map/ppermute | solution.py:227

commit v4 on v3

--- a/solution.py
+++ b/solution.py
@@ -68,6 +68,30 @@
         compiler_params=pltpu.CompilerParams(vmem_limit_bytes=56 * 2**20),
         name="pack",
     )(queries, keys, values)
+
+
+def unpack(back, heads):
+    _, tokens, _ = back.shape
+
+    def kernel(back_ref, o_ref, sems):
+        copies = [
+            pltpu.make_async_copy(back_ref.at[h], o_ref.at[0, :, h * HEAD : (h + 1) * HEAD], sems.at[h])
+            for h in range(heads)
+        ]
+        for copy in copies:
+            copy.start()
+        for copy in copies:
+            copy.wait()
+
+    return pl.pallas_call(
+        kernel,
+        out_shape=jax.ShapeDtypeStruct((1, tokens, heads * HEAD), back.dtype),
+        in_specs=[pl.BlockSpec(memory_space=pl.ANY)],
+        out_specs=pl.BlockSpec(memory_space=pl.ANY),
+        scratch_shapes=[pltpu.SemaphoreType.DMA((heads,))],
+        compiler_params=pltpu.CompilerParams(vmem_limit_bytes=16 * 2**20),
+        name="unpack",
+    )(back)
 
 
 def attend(lengths, span_mask, place, got, other):
@@ -227,8 +251,8 @@
     other = lax.ppermute(got[:, 1:], "core", [(0, 1), (1, 0)])
     active = (lax.axis_index(CHIPS) < heads).astype(jnp.int32)
     out = attend(lengths, span_mask, jnp.stack([active, core]), got, other)
-    back = lax.all_to_all(out.reshape(chips, tokens, HEAD), CHIPS, 0, 0, tiled=True)[:heads]
-    return jnp.transpose(back, (1, 0, 2)).reshape(1, tokens, width)
+    back = lax.all_to_all(out.reshape(chips, tokens, HEAD), CHIPS, 0, 0, tiled=True)
+    return unpack(back, heads)
 
 
 def solution(mesh):

time: 150 us -> 153 us (1.020); the launches traced: 153 us -> 154 us
  Pallas kernels: 39.1 us -> 42 us
  local copies, waits for them, and re-layouts: 4.94 us -> 3.05 us
where the time goes in v4:
time: 153 us; the launch traced here: 154 us
  blocking collectives  103 us (67%)
  Pallas kernels  42 us (27%)
  waiting for transfers between devices  5.79 us (4%)
  local copies, waits for them, and re-layouts  3.05 us (2%)
    all_to_all x1, blocking collectives, body(): got = lax.all_to_all(sent, CHIPS, 0, 0, tiled=True)  70.5 us
    pallas_call x1, Pallas kernels, attend(): pl.pallas_call(kernel, out_shape=jax.ShapeDtypeStruct((groups, rows, HEAD...  37.5 us
    all_to_all x1, blocking collectives, body(): lax.all_to_all(out.reshape(chips, tokens, HEAD), CHIPS, 0, 0, tiled=True)  32.2 us
    ppermute x1, waiting for transfers between devices, body(): other = lax.ppermute(got[:, 1:], 'core', [(0, 1), (1, 0)])  5.79 us
    pallas_call x1, Pallas kernels, pack(): pl.pallas_call(kernel, out_shape=jax.ShapeDtypeStruct((slots, 3, tokens,...  3.08 us
  transfers between devices with their start and end apart: 1, of which 1 were waited for; matrix products, arithmetic and copies ran while one was open for 0% of the time, Pallas kernels for 0%

profile of v4, /device:TPU:0, one launch (start us, length us, event | category | flops | bytes accessed | tf_op | source)
XLA Modules:
  0.0 153.7 jit_solution(12431308401879271928)
XLA Ops:
  0.0 3.1 %pack.1 = bf16[64,3,96,128]{3,2,1,0:T(8,128)(2,1)} custom-call(bf16[1,96,6144]{2,1,0:T(8,128)(2,1)} %q_ref.1, bf16[1,96,6144]{2,1,0:T(8,128)(2,1)} %k_ref.1, bf16[1,96,6144]{2,1,0:T(8,128)(2,1)} %v_ref.1), custom_call_target="tpu_custom_call" | custom-call | tf_op jit(solution)/shard_map/pack/pallas_call | solution.py:57
  3.1 70.5 %all_to_all.10.got_ref = bf16[64,3,96,128]{3,2,1,0:T(8,128)(2,1)S(1)} all-to-all(bf16[64,3,96,128]{3,2,1,0:T(8,128)(2,1)} %pack.1), channel_id=1, replica_groups=mesh['xh'=2,'z'=4,'xl'=2,'y'=4,'core'=2] {'xh','z','xl','y'}, dimensions={0} | all-to-all | bytes 9437184 | tf_op jit(solution)/shard_map/all_to_all | solution.py:249
  73.5 0.0 copy-start.2
  73.5 0.0 copy-start
  73.5 0.0 copy-start.1
  73.6 2.4 %slice.4 = bf16[64,2,96,128]{3,2,1,0:T(8,128)(2,1)} slice(bf16[64,3,96,128]{3,2,1,0:T(8,128)(2,1)S(1)} %all_to_all.10.got_ref), slice={[0:64], [1:3], [0:96], [0:128]} | slice | bytes 6291456 | tf_op jit(solution)/shard_map/slice | solution.py:251
  75.9 0.7 copy-done.2
  76.6 0.0 collective-permute-start
  76.6 0.1 pad_add_fusion.place_ref
  76.7 5.8 %collective-permute-done.other_ref = bf16[64,2,96,128]{3,2,1,0:T(8,128)(2,1)S(1)} collective-permute-done((bf16[64,2,96,128]{3,2,1,0:T(8,128)(2,1)}, bf16[64,2,96,128]{3,2,1,0:T(8,128)(2,1)S(1)}, u32[]{:S(2)}, u32[]{:S(2)}) %collective-permute-start) | collective-permute-done | bytes 3145760 | tf_op jit(solution)/shard_map/ppermute | solution.py:251
  82.5 0.0 copy-done
  82.5 0.0 copy-done.1
  82.5 37.5 %attend.1 = bf16[8,768,128]{2,1,0:T(8,128)(2,1)S(1)} custom-call(s32[8]{0:T(128)S(1)} %copy-done.1, s32[8,8]{1,0:T(8,128)S(1)} %copy-done, s32[2]{0:T(128)S(1)} %pad_add_fusion.place_ref, bf16[64,3,96,128]{3,2,1,0:T(8,128)(2,1)} %copy-done.2, bf16[64,2,96,128]{3,2,1,0:T(8,128)(2,1)S(1)} %collective-permute-done.other_ref), custom_call_target="tpu_custom_call" | custom-call | tf_op jit(solution)/shard_map/attend/pallas_call | solution.py:218
  120.0 32.2 %all_to_all.11.back_ref = bf16[64,96,128]{2,1,0:T(8,128)(2,1)S(1)} all-to-all(bf16[64,96,128]{2,1,0:T(8,128)(2,1)S(1)} %bitcast.3), channel_id=1, replica_groups=mesh['xh'=2,'z'=4,'xl'=2,'y'=4,'core'=2] {'xh','z','xl','y'}, dimensions={0} | all-to-all | bytes 3145728 | tf_op jit(solution)/shard_map/all_to_all | solution.py:254
  152.1 1.4 unpack.1
Async XLA Ops:
  73.5 3.0 %copy-start.2 = (bf16[64,3,96,128]{3,2,1,0:T(8,128)(2,1)}, bf16[64,3,96,128]{3,2,1,0:T(8,128)(2,1)S(1)}, u32[]{:S(2)}) copy-start(bf16[64,3,96,128]{3,2,1,0:T(8,128)(2,1)S(1)} %all_to_all.10.got_ref) | copy-start | bytes 14155780
  73.5 8.9 %copy-start = (s32[8,8]{1,0:T(8,128)S(1)}, s32[8,8]{1,0:T(8,128)}, u32[]{:S(2)}) copy-start(s32[8,8]{1,0:T(8,128)} %mask_ref.1) | copy-start | bytes 772
  73.5 8.9 %copy-start.1 = (s32[8]{0:T(128)S(1)}, s32[8]{0:T(128)}, u32[]{:S(2)}) copy-start(s32[8]{0:T(128)} %len_ref.1) | copy-start | bytes 100
  76.6 5.9 %collective-permute-start = (bf16[64,2,96,128]{3,2,1,0:T(8,128)(2,1)}, bf16[64,2,96,128]{3,2,1,0:T(8,128)(2,1)S(1)}, u32[]{:S(2)}, u32[]{:S(2)}) collective-permute-start(bf16[64,2,96,128]{3,2,1,0:T(8,128)(2,1)} %slice.4), channel_id=1, source_target_pairs={{0,1},{1,0},{2,3},{3,2},{4,5},{5,4},{6,7},{7,6},{8,9},{9,8},{10,11... | collective-permute-start | bytes 9437192 | tf_op jit(solution)/shard_map/ppermute | solution.py:251

commit v5 on v4

--- a/solution.py
+++ b/solution.py
@@ -68,6 +68,27 @@
         compiler_params=pltpu.CompilerParams(vmem_limit_bytes=56 * 2**20),
         name="pack",
     )(queries, keys, values)
+
+
+def tail(got):
+    slots, kinds, tokens, _ = got.shape
+
+    def kernel(got_ref, o_ref):
+        def one(i, carry):
+            for j in range(4):
+                o_ref[i * 4 + j] = got_ref[i * 4 + j, 1:]
+            return carry
+
+        lax.fori_loop(0, slots // 4, one, 0)
+
+    return pl.pallas_call(
+        kernel,
+        out_shape=jax.ShapeDtypeStruct((slots, kinds - 1, tokens, HEAD), got.dtype),
+        in_specs=[pl.BlockSpec(memory_space=pltpu.VMEM)],
+        out_specs=pl.BlockSpec(memory_space=pltpu.VMEM),
+        compiler_params=pltpu.CompilerParams(vmem_limit_bytes=16 * 2**20),
+        name="tail",
+    )(got)
 
 
 def unpack(back, heads):
@@ -248,7 +269,7 @@
     sent = pack(queries, keys, values, chips)
     got = lax.all_to_all(sent, CHIPS, 0, 0, tiled=True)
 
-    other = lax.ppermute(got[:, 1:], "core", [(0, 1), (1, 0)])
+    other = lax.ppermute(tail(got), "core", [(0, 1), (1, 0)])
     active = (lax.axis_index(CHIPS) < heads).astype(jnp.int32)
     out = attend(lengths, span_mask, jnp.stack([active, core]), got, other)
     back = lax.all_to_all(out.reshape(chips, tokens, HEAD), CHIPS, 0, 0, tiled=True)

time: 153 us -> 148 us (0.967); the launches traced: 154 us -> 147 us
  Pallas kernels: 42 us -> 37.1 us
  local copies, waits for them, and re-layouts: 3.05 us -> 1 us
    pallas_call x1, Pallas kernels: 37.5 us -> 30.5 us  [attend(): pl.pallas_call(kernel, out_shape=jax.ShapeDtypeStruct((groups, rows, HEAD...]
    slice x1 -> x0, local copies, waits for them, and re-layouts: 2.39 us -> none  [body(): other = lax.ppermute(got[:, 1:], 'core', [(0, 1), (1, 0)])]
    pallas_call x0 -> x1, Pallas kernels: none -> 2.05 us  [tail(): pl.pallas_call(kernel, out_shape=jax.ShapeDtypeStruct((slots, kinds - 1,...]
where the time goes in v5:
time: 148 us; the launch traced here: 147 us
  blocking collectives  103 us (70%)
  Pallas kernels  37.1 us (25%)
  waiting for transfers between devices  5.79 us (4%)
    all_to_all x1, blocking collectives, body(): got = lax.all_to_all(sent, CHIPS, 0, 0, tiled=True)  70.5 us
    all_to_all x1, blocking collectives, body(): lax.all_to_all(out.reshape(chips, tokens, HEAD), CHIPS, 0, 0, tiled=True)  32.1 us
    pallas_call x1, Pallas kernels, attend(): pl.pallas_call(kernel, out_shape=jax.ShapeDtypeStruct((groups, rows, HEAD...  30.5 us
    ppermute x1, waiting for transfers between devices, body(): other = lax.ppermute(tail(got), 'core', [(0, 1), (1, 0)])  5.79 us
    pallas_call x1, Pallas kernels, pack(): pl.pallas_call(kernel, out_shape=jax.ShapeDtypeStruct((slots, 3, tokens,...  3.08 us
  transfers between devices with their start and end apart: 1, of which 1 were waited for; matrix products, arithmetic and copies ran while one was open for 0% of the time, Pallas kernels for 0%

profile of v5, /device:TPU:0, one launch (start us, length us, event | category | flops | bytes accessed | tf_op | source)
XLA Modules:
  0.0 146.8 jit_solution(185526902981129157)
XLA Ops:
  0.0 3.1 %pack.1 = bf16[64,3,96,128]{3,2,1,0:T(8,128)(2,1)} custom-call(bf16[1,96,6144]{2,1,0:T(8,128)(2,1)} %q_ref.1, bf16[1,96,6144]{2,1,0:T(8,128)(2,1)} %k_ref.1, bf16[1,96,6144]{2,1,0:T(8,128)(2,1)} %v_ref.1), custom_call_target="tpu_custom_call" | custom-call | tf_op jit(solution)/shard_map/pack/pallas_call | solution.py:57
  3.1 70.5 %all_to_all.10.got_ref = bf16[64,3,96,128]{3,2,1,0:T(8,128)(2,1)S(1)} all-to-all(bf16[64,3,96,128]{3,2,1,0:T(8,128)(2,1)} %pack.1), channel_id=1, replica_groups=mesh['xh'=2,'z'=4,'xl'=2,'y'=4,'core'=2] {'xh','z','xl','y'}, dimensions={0} | all-to-all | bytes 9437184 | tf_op jit(solution)/shard_map/all_to_all | solution.py:270
  73.5 0.0 copy-start
  73.5 0.0 copy-start.1
  73.5 0.0 copy-start.2
  73.6 2.1 %tail.1 = bf16[64,2,96,128]{3,2,1,0:T(8,128)(2,1)} custom-call(bf16[64,3,96,128]{3,2,1,0:T(8,128)(2,1)S(1)} %all_to_all.10.got_ref), custom_call_target="tpu_custom_call" | custom-call | tf_op jit(solution)/shard_map/tail/pallas_call | solution.py:84
  75.6 1.0 copy-done
  76.6 0.0 collective-permute-start
  76.6 0.1 pad_add_fusion.place_ref
  76.7 5.8 %collective-permute-done.other_ref = bf16[64,2,96,128]{3,2,1,0:T(8,128)(2,1)S(1)} collective-permute-done((bf16[64,2,96,128]{3,2,1,0:T(8,128)(2,1)}, bf16[64,2,96,128]{3,2,1,0:T(8,128)(2,1)S(1)}, u32[]{:S(2)}, u32[]{:S(2)}) %collective-permute-start) | collective-permute-done | bytes 3145760 | tf_op jit(solution)/shard_map/ppermute | solution.py:272
  82.5 0.0 copy-done.1
  82.5 0.0 copy-done.2
  82.5 30.5 %attend.1 = bf16[8,768,128]{2,1,0:T(8,128)(2,1)S(1)} custom-call(s32[8]{0:T(128)S(1)} %copy-done.2, s32[8,8]{1,0:T(8,128)S(1)} %copy-done.1, s32[2]{0:T(128)S(1)} %pad_add_fusion.place_ref, bf16[64,3,96,128]{3,2,1,0:T(8,128)(2,1)} %copy-done, bf16[64,2,96,128]{3,2,1,0:T(8,128)(2,1)S(1)} %collective-permute-done.other_ref), custom_call_target="tpu_custom_call" | custom-call | tf_op jit(solution)/shard_map/attend/pallas_call | solution.py:239
  113.0 32.1 %all_to_all.11.back_ref = bf16[64,96,128]{2,1,0:T(8,128)(2,1)S(1)} all-to-all(bf16[64,96,128]{2,1,0:T(8,128)(2,1)S(1)} %bitcast.3), channel_id=1, replica_groups=mesh['xh'=2,'z'=4,'xl'=2,'y'=4,'core'=2] {'xh','z','xl','y'}, dimensions={0} | all-to-all | bytes 3145728 | tf_op jit(solution)/shard_map/all_to_all | solution.py:275
  145.2 1.4 unpack.1
Async XLA Ops:
  73.5 3.1 %copy-start = (bf16[64,3,96,128]{3,2,1,0:T(8,128)(2,1)}, bf16[64,3,96,128]{3,2,1,0:T(8,128)(2,1)S(1)}, u32[]{:S(2)}) copy-start(bf16[64,3,96,128]{3,2,1,0:T(8,128)(2,1)S(1)} %all_to_all.10.got_ref) | copy-start | bytes 14155780
  73.5 8.9 %copy-start.1 = (s32[8,8]{1,0:T(8,128)S(1)}, s32[8,8]{1,0:T(8,128)}, u32[]{:S(2)}) copy-start(s32[8,8]{1,0:T(8,128)} %mask_ref.1) | copy-start | bytes 772
  73.5 8.9 %copy-start.2 = (s32[8]{0:T(128)S(1)}, s32[8]{0:T(128)}, u32[]{:S(2)}) copy-start(s32[8]{0:T(128)} %len_ref.1) | copy-start | bytes 100
  76.6 5.9 %collective-permute-start = (bf16[64,2,96,128]{3,2,1,0:T(8,128)(2,1)}, bf16[64,2,96,128]{3,2,1,0:T(8,128)(2,1)S(1)}, u32[]{:S(2)}, u32[]{:S(2)}) collective-permute-start(bf16[64,2,96,128]{3,2,1,0:T(8,128)(2,1)} %tail.1), channel_id=1, source_target_pairs={{0,1},{1,0},{2,3},{3,2},{4,5},{5,4},{6,7},{7,6},{8,9},{9,8},{10,11... | collective-permute-start | bytes 9437192 | tf_op jit(solution)/shard_map/ppermute | solution.py:272
